TPU v7x, 32 devices: a whole 2x2x4 slice. The times are simulated.
32 devices in a mesh: ctx: 16 (over z, y, x), tp: 2 (over core).
Axes of the slice: x: 2, y: 2, z: 4, core: 2. Of those that a mesh axis runs over, the one named last changes fastest.
Arguments:
- tokens: bfloat16 [16384, 1536], P('ctx'), may hold values from -6 to 6
- w_query: bfloat16 [1536, 1536], P(None, 'tp'), may hold values from -0.15625 to 0.15625
- w_key: bfloat16 [1536, 1536], P(None, 'tp'), may hold values from -0.15625 to 0.15625
- w_value: bfloat16 [1536, 1536], P(None, 'tp'), may hold values from -0.15625 to 0.15625
- w_out: bfloat16 [1536, 1536], P('tp'), may hold values from -0.15625 to 0.15625
Outputs:
- mixed: bfloat16 [16384, 1536], P('ctx', 'tp')
All inputs are finite; a program needn't handle non-finite values.
Results may differ from a plain program's by a relative error of at most 0.0071.
Values may be sent and summed in bfloat16 or wider, within the bound.
A program may use at most 128 MiB of HBM per device.

v0:
```python
import jax
import jax.numpy as jnp
from jax import lax
from jax.sharding import PartitionSpec as P

HDIM = 128
BLK = 512


def carried_in(part, axis, combine, identity):
    place = lax.axis_index(axis)
    gathered = lax.all_gather(part, axis)
    state = jnp.zeros_like(part) + jnp.asarray(identity, part.dtype)

    def one(lap, state):
        return combine(state, lax.dynamic_index_in_dim(gathered, lap, 0, False))

    return lax.fori_loop(0, place, one, state)


def add_states(earlier, later):
    return earlier + later


def body(tokens, w_query, w_key, w_value, w_out):
    tok_rows = tokens.shape[0]
    count = tok_rows // BLK
    heads_here = w_query.shape[1] // HDIM
    query = jax.nn.silu(jnp.dot(tokens, w_query, preferred_element_type=jnp.float32)).astype(
        jnp.bfloat16
    )
    keys = jax.nn.silu(jnp.dot(tokens, w_key, preferred_element_type=jnp.float32)).astype(
        jnp.bfloat16
    )
    values = jnp.dot(tokens, w_value, preferred_element_type=jnp.float32).astype(jnp.bfloat16)
    query = query.reshape(count, BLK, heads_here, HDIM)
    keys = keys.reshape(count, BLK, heads_here, HDIM)
    values = values.reshape(count, BLK, heads_here, HDIM)
    block_state = jnp.einsum("bshd,bshe->bhde", keys, values, preferred_element_type=jnp.float32)
    total = jnp.sum(block_state, axis=0)
    zeros_state = jnp.zeros_like(total)
    prefix = carried_in(total, "ctx", add_states, zeros_state)
    running = jnp.cumsum(block_state, axis=0)
    within = jnp.concatenate([jnp.zeros_like(block_state[:1]), running[:-1]], axis=0)
    carried = (prefix[None] + within).astype(jnp.bfloat16)
    causal = jnp.tril(jnp.ones((BLK, BLK), dtype=bool))
    scores = jnp.einsum("bshd,bthd->bhst", query, keys, preferred_element_type=jnp.float32)
    scores = jnp.where(causal[None, None], scores, 0.0).astype(jnp.bfloat16)
    attended = jnp.einsum("bhst,bthe->bshe", scores, values, preferred_element_type=jnp.float32)
    attended = attended + jnp.einsum(
        "bshd,bhde->bshe", query, carried, preferred_element_type=jnp.float32
    )
    meansq = jnp.mean(attended * attended, axis=-1, keepdims=True)
    normed = (
        (attended * lax.rsqrt(meansq + 1e-06))
        .astype(jnp.bfloat16)
        .reshape(tok_rows, heads_here * HDIM)
    )
    partial_out = jnp.dot(normed, w_out, preferred_element_type=jnp.float32)
    mixed = lax.psum_scatter(partial_out, "tp", scatter_dimension=1, tiled=True).astype(
        jnp.bfloat16
    )
    return mixed


def solution(mesh):
    return jax.shard_map(
        body,
        mesh=mesh,
        in_specs=(P("ctx", None), P(None, "tp"), P(None, "tp"), P(None, "tp"), P("tp", None)),
        out_specs=P("ctx", "tp"),
        check_vma=False,
    )
```

profile of v0, /device:TPU:0, one launch (start us, length us, event | category | flops | bytes accessed | tf_op | source)
XLA Modules:
  0.0 185.5 jit_solution(5648767403875890950)
XLA Ops:
  6.5 0.0 copy-start
  6.5 0.0 all-gather.3.cloned.1.call-start
  6.5 1.9 %copy-done = bf16[1024,1536]{1,0:T(8,128)(2,1)S(1)} copy-done((bf16[1024,1536]{1,0:T(8,128)(2,1)S(1)}, bf16[1024,1536]{1,0:T(8,128)(2,1)}, u32[]{:S(2)}) %copy-start) | copy-done | bytes 3145752
  8.4 5.6 %multiply_convert_fusion = bf16[1024,768]{1,0:T(8,128)(2,1)} fusion(bf16[1024,1536]{1,0:T(8,128)(2,1)S(1)} %copy-done, bf16[1536,768]{1,0:T(8,128)(2,1)} %param.9), kind=kOutput, calls=%fused_computation.10 | convolution fusion | flops 2419851264 | bytes 7077888 | tf_op jit(solution)/shard_map/dot_general | solution.py:32
  14.0 4.3 %reshape.35 = bf16[2,512,6,128]{3,2,1,0:T(8,128)(2,1)} reshape(bf16[1024,768]{1,0:T(8,128)(2,1)} %multiply_convert_fusion) | data formatting | bytes 3145728 | tf_op jit(solution)/shard_map/reshape | solution.py:37
  18.4 4.1 %copy.26 = bf16[2,512,6,128]{1,3,2,0:T(8,128)(2,1)} copy(bf16[2,512,6,128]{3,2,1,0:T(8,128)(2,1)} %reshape.35) | data formatting | bytes 3145728 | tf_op jit(solution)/shard_map/reshape | solution.py:37
  22.5 5.3 %convolution_convert_fusion = bf16[1024,768]{1,0:T(8,128)(2,1)} fusion(bf16[1024,1536]{1,0:T(8,128)(2,1)S(1)} %copy-done, bf16[1536,768]{1,0:T(8,128)(2,1)} %param.10), kind=kOutput, calls=%fused_computation.13 | convolution fusion | flops 2416705536 | bytes 7077888 | tf_op jit(solution)/shard_map/dot_general | solution.py:35
  27.8 4.3 %reshape.34 = bf16[2,512,6,128]{3,2,1,0:T(8,128)(2,1)} reshape(bf16[1024,768]{1,0:T(8,128)(2,1)} %convolution_convert_fusion) | data formatting | bytes 3145728 | tf_op jit(solution)/shard_map/reshape | solution.py:38
  32.1 4.4 %fusion.16 = (f32[6,128,128]{2,1,0:T(8,128)}, f32[2,6,128,128]{3,2,1,0:T(8,128)}) fusion(bf16[2,512,6,128]{1,3,2,0:T(8,128)(2,1)} %copy.26, bf16[2,512,6,128]{3,2,1,0:T(8,128)(2,1)} %reshape.34), kind=kOutput, calls=%fused_computation.25 | convolution fusion | flops 201424896 | bytes 4325376 | tf_op jit(solution)/shard_map/bshd,bshe->bhde/dot_general | solution.py:39
  36.5 0.0 all-gather.3.cloned.1.call-update
  36.5 0.0 reduce-scatter.2.cloned.1.call-start
  36.6 5.6 %multiply_convert_fusion.1 = bf16[1024,768]{1,0:T(8,128)(2,1)} fusion(bf16[1024,1536]{1,0:T(8,128)(2,1)S(1)} %copy-done, bf16[1536,768]{1,0:T(8,128)(2,1)} %param.8), kind=kOutput, calls=%fused_computation.11 | convolution fusion | flops 2419851264 | bytes 7077888 | tf_op jit(solution)/shard_map/dot_general | solution.py:29
  42.2 4.3 %reshape.33 = bf16[2,512,6,128]{3,2,1,0:T(8,128)(2,1)} reshape(bf16[1024,768]{1,0:T(8,128)(2,1)} %multiply_convert_fusion.1) | data formatting | bytes 3145728 | tf_op jit(solution)/shard_map/reshape | solution.py:36
  46.6 1.2 fusion.17
  47.8 0.8 slice.4
  48.6 0.1 iota_compare_fusion
  48.6 8.3 %fusion = f32[2,6,128,512]{3,2,1,0:T(8,128)} fusion(pred[512,512]{1,0:T(8,128)(4,1)S(1)} %iota_compare_fusion, bf16[2,512,6,128]{1,3,2,0:T(8,128)(2,1)} %copy.26, bf16[2,512,6,128]{3,2,1,0:T(8,128)(2,1)} %reshape.34, bf16[2,512,6,128]{3,2,1,0:T(8,128)(2,1)} %reshape.33), kind=kOutput, calls=%fused_computation.2 | convolution fusion | flops 1616904192 | bytes 8126464 | tf_op jit(solution)/shard_map/bhst,bthe->bshe/dot_general | solution.py:49
  56.9 76.7 %all-gather.3.cloned.1.call-done = f32[96,128,128]{2,1,0:T(8,128)} async-done(((f32[6,128,128]{2,1,0:T(8,128)}), f32[96,128,128]{2,1,0:T(8,128)}) %all-gather.3.cloned.1.call-update) | async-done | bytes 6291472 | tf_op jit(solution)/shard_map/all_gather | solution.py:12
  133.6 0.2 while.10
  133.8 3.5 %fusion.5 = (f32[2,512,6]{1,2,0:T(8,128)S(1)}, f32[2,6,128,512]{3,2,1,0:T(8,128)S(1)}) fusion(f32[2,6,128,512]{3,2,1,0:T(8,128)} %fusion, bf16[2,512,6,128]{3,2,1,0:T(8,128)(2,1)} %reshape.33, f32[1,6,128,128]{3,2,1,0:T(8,128)} %slice.4, f32[6,128,128]{2,1,0:T(8,128)S(1)} %get-tuple-element.28), kind=kOutput, calls=%fused_computation.8 | convolution fusion | flops 204072960 | bytes 8675328 | tf_op jit(solution)/shard_map/bshd,bhde->bshe/dot_general | solution.py:50
  137.3 0.5 fusion.6
  137.8 1.6 copy.30
  139.4 0.0 copy-start.1
  139.4 0.4 copy.38
  139.9 1.2 copy-done.1
  141.1 4.6 %fusion.18 = f32[1024,1536]{1,0:T(8,128)} fusion(bf16[1024,768]{0,1:T(8,128)(2,1)S(1)} %bitcast.29, bf16[768,1536]{1,0:T(8,128)(2,1)S(1)} %copy-done.1), kind=kOutput, calls=%fused_computation.27 | convolution fusion | flops 2415919104 | bytes 10223616 | tf_op jit(solution)/shard_map/dot_general | solution.py:59
  145.7 0.0 reduce-scatter.2.cloned.1.call-update
  145.8 29.7 %reduce-scatter.2.cloned.1.call-done = f32[1024,768]{1,0:T(8,128)} async-done(((f32[1024,1536]{1,0:T(8,128)}), f32[1024,768]{1,0:T(8,128)}) %reduce-scatter.2.cloned.1.call-update) | async-done | bytes 3145744 | tf_op jit(solution)/shard_map/reduce_scatter | solution.py:60
  175.5 3.2 %convert_element_type.27 = bf16[1024,768]{1,0:T(8,128)(2,1)} convert(f32[1024,768]{1,0:T(8,128)} %reduce-scatter.2.cloned.1.call-done) | non-fusion elementwise | flops 786432 | bytes 4718592 | tf_op jit(solution)/shard_map/convert_element_type | solution.py:60
  (2 shorter events, 0.0 us)
Async XLA Ops:
  6.5 1.9 %copy-start = (bf16[1024,1536]{1,0:T(8,128)(2,1)S(1)}, bf16[1024,1536]{1,0:T(8,128)(2,1)}, u32[]{:S(2)}) copy-start(bf16[1024,1536]{1,0:T(8,128)(2,1)} %param.7) | copy-start | bytes 9437188
  6.5 127.0 %all-gather.3.cloned.1.call-start = ((), (), s32[]{:S(2)}) async-start(), calls=%async_computation.2 | async-start | bytes 6684672 | tf_op jit(solution)/shard_map/all_gather | solution.py:12
  36.5 138.9 %reduce-scatter.2.cloned.1.call-start = ((), (), s32[]{:S(2)}) async-start(), calls=%async_computation.1 | async-start | bytes 9437184 | tf_op jit(solution)/shard_map/reduce_scatter | solution.py:60
  139.4 1.7 copy-start.1
Sparse Core Ops, SparseCore 0:
  36.7 96.8 all-gather.2
  145.9 29.5 reduce-scatter.1
where the time goes:
time: 187 us; the launch traced here: 186 us
  waiting for transfers between devices  106 us (57%)
  matrix products  37.3 us (20%)
  local copies, waits for them, and re-layouts  23 us (12%)
  between operations  13.5 us (7%)
  other arithmetic  4.99 us (3%)
    all_gather x1, waiting for transfers between devices, carried_in(): gathered = lax.all_gather(part, axis)  76.7 us
    reduce_scatter x1, waiting for transfers between devices, body(): lax.psum_scatter(partial_out, 'tp', scatter_dimension=1, tiled=True)  29.7 us
    reshape x2, local copies, waits for them, and re-layouts, body(): keys = keys.reshape(count, BLK, heads_here, HDIM)  8.41 us
    dot_general x1, matrix products, body(): jnp.einsum('bhst,bthe->bshe', scores, values, preferred_element_type=jnp....  8.26 us
    dot_general x1, matrix products, body(): jnp.dot(tokens, w_query, preferred_element_type=jnp.float32)  5.63 us
    dot_general x1, matrix products, body(): jnp.dot(tokens, w_key, preferred_element_type=jnp.float32)  5.61 us
    dot_general x1, matrix products, body(): jnp.dot(tokens, w_value, preferred_element_type=jnp.float32)  5.35 us
    dot_general x1, matrix products, body(): partial_out = jnp.dot(normed, w_out, preferred_element_type=jnp.float32)  4.63 us
  transfers between devices with their start and end apart: 2, of which 2 were waited for; matrix products, arithmetic and copies ran while one was open for 11% of the time, Pallas kernels for 0%

commit v1 on v0

v1 whole, which is shorter than its diff:
```python
import functools

import jax
import jax.numpy as jnp
from jax import lax
from jax.experimental import pallas as pl
from jax.experimental.pallas import tpu as pltpu
from jax.sharding import PartitionSpec as P

HDIM = 128
PAIR = 2 * HDIM
CHUNK = 256
TILE = 512
GROUP = 4
MESH = pl.DeviceIdType.MESH
F32 = jnp.float32
BF16 = jnp.bfloat16


def silu(u):
    return u * (0.5 * jnp.tanh(0.5 * u) + 0.5)


def dot(a, b):
    return jnp.dot(a, b, preferred_element_type=F32)


def kernel(
    n_ctx,
    tok_hbm,
    wq_hbm,
    wk_hbm,
    wv_hbm,
    wo_hbm,
    out_hbm,
    tok,
    wq,
    wk,
    wv,
    wo_own,
    wo_peer,
    q_v,
    k_v,
    v_v,
    att,
    within,
    run,
    normed,
    normed_peer,
    acc,
    out_v,
    p1_send,
    p1_recv,
    p2_send,
    p2_recv,
    p3_send,
    p3_recv,
    tok_sem,
    w_sem,
    wo_sem,
    out_sem,
    wo_ssem,
    wo_rsem,
    s1,
    r1,
    s2,
    r2,
    s3,
    r3,
    sn,
    rn,
):
    rows = tok.shape[0]
    tiles = rows // TILE
    per_tile = TILE // CHUNK
    cols = wq.shape[1]
    pairs = cols // PAIR
    out_cols = wo_own.shape[1]
    groups = n_ctx // GROUP
    me = lax.axis_index("ctx")
    t = lax.axis_index("tp")
    g = me // GROUP
    p = lax.rem(me, GROUP)
    peer = 1 - t

    barrier = pltpu.get_barrier_semaphore()
    for k in range(1, GROUP):
        pl.semaphore_signal(
            barrier,
            inc=1,
            device_id={"ctx": g * GROUP + lax.rem(p + k, GROUP)},
            device_id_type=MESH,
        )
    for k in range(1, groups):
        pl.semaphore_signal(
            barrier,
            inc=1,
            device_id={"ctx": lax.rem(g + k, groups) * GROUP + p},
            device_id_type=MESH,
        )
    pl.semaphore_signal(barrier, inc=1, device_id={"tp": peer}, device_id_type=MESH)

    def tok_copy(r):
        part = pl.ds(r * TILE, TILE)
        return pltpu.make_async_copy(tok_hbm.at[part], tok.at[part], tok_sem.at[r])

    def w_copy(which, i):
        part = pl.ds(i * PAIR, PAIR)
        src, dst = ((wk_hbm, wk), (wv_hbm, wv), (wq_hbm, wq))[which]
        return pltpu.make_async_copy(
            src.at[:, part], dst.at[:, part], w_sem.at[which, i]
        )

    def wo_cols(side):
        return pl.ds(pl.multiple_of(side * out_cols, 128), out_cols)

    wo_copy = pltpu.make_async_copy(wo_hbm.at[:, wo_cols(t)], wo_own, wo_sem)
    wo_remote = pltpu.make_async_remote_copy(
        src_ref=wo_hbm.at[:, wo_cols(peer)],
        dst_ref=wo_peer,
        send_sem=wo_ssem,
        recv_sem=wo_rsem,
        device_id={"tp": peer},
        device_id_type=MESH,
    )

    w_copy(0, 0).start()
    tok_copy(0).start()
    w_copy(1, 0).start()
    for r in range(1, tiles):
        tok_copy(r).start()
    for i in range(1, pairs):
        w_copy(0, i).start()
        w_copy(1, i).start()
    for i in range(pairs):
        w_copy(2, i).start()
    wo_copy.start()

    def p1_copy(i, k, slot, to):
        return pltpu.make_async_remote_copy(
            src_ref=p1_send.at[i, to],
            dst_ref=p1_recv.at[i, slot],
            send_sem=s1.at[i, k],
            recv_sem=r1.at[i, k],
            device_id={"ctx": g * GROUP + to},
            device_id_type=MESH,
        )

    def p2_copy(i, slot, to):
        return pltpu.make_async_remote_copy(
            src_ref=p2_send.at[i],
            dst_ref=p2_recv.at[i, slot],
            send_sem=s2.at[i, to],
            recv_sem=r2.at[i, slot],
            device_id={"ctx": to * GROUP + p},
            device_id_type=MESH,
        )

    def p3_copy(i, k, slot, to):
        return pltpu.make_async_remote_copy(
            src_ref=p3_send.at[i, to],
            dst_ref=p3_recv.at[i, slot],
            send_sem=s3.at[i, k],
            recv_sem=r3.at[i, k],
            device_id={"ctx": g * GROUP + to},
            device_id_type=MESH,
        )

    def after(k):
        return lax.rem(p + k, GROUP)

    def before(k):
        return lax.rem(p + GROUP - k, GROUP)

    def p1_start(i):
        p1_send[i] = run[...].astype(BF16).reshape(GROUP, PAIR // GROUP, HDIM)
        p1_recv[i, p] = p1_send[i, p]
        for k in range(1, GROUP):
            p1_copy(i, k, p, after(k)).start()

    def p1_finish(i):
        for k in range(1, GROUP):
            p1_copy(i, k, before(k), after(k)).wait_recv()
        total = p1_recv[i, 0].astype(F32)
        for j in range(1, GROUP):
            total = total + p1_recv[i, j].astype(F32)
        p2_send[i] = total.astype(BF16)
        for to in range(1, groups):

            @pl.when(to > g)
            def _():
                p2_copy(i, g, to).start()

    def p2_finish(i):
        base = run.at[pl.ds(0, PAIR // GROUP)]
        base[...] = jnp.zeros_like(base)
        for frm in range(groups - 1):

            @pl.when(frm < g)
            def _():
                p2_copy(i, frm, frm).wait_recv()
                base[...] += p2_recv[i, frm].astype(F32)

        prefix = base[...]
        for j in range(GROUP):
            p3_send[i, j] = prefix.astype(BF16)
            if j < GROUP - 1:
                prefix = prefix + p1_recv[i, j].astype(F32)
        p3_recv[i, p] = p3_send[i, p]
        for k in range(1, GROUP):
            p3_copy(i, k, p, after(k)).start()

    def p3_finish(i):
        for k in range(1, GROUP):
            p3_copy(i, k, before(k), after(k)).wait_recv()

    def tile_rows(r):
        return pl.ds(pl.multiple_of(r * TILE, TILE), TILE)

    def kv_stage(i):
        cs = slice(i * PAIR, (i + 1) * PAIR)
        w_copy(0, i).wait()
        for r in range(tiles):
            if i == 0:
                tok_copy(r).wait()
            rs = slice(r * TILE, (r + 1) * TILE)
            keys = silu(dot(tok[rs, :], wk[:, cs])).astype(BF16)
            k_v[rs, cs] = keys
            if r == 0:
                w_copy(1, i).wait()
            vals = dot(tok[rs, :], wv[:, cs]).astype(BF16)
            v_v[rs, cs] = vals
            for c in range(per_tile):
                at = slice(c * CHUNK, (c + 1) * CHUNK)
                both = lax.dot_general(
                    keys[at],
                    vals[at],
                    (((0,), (0,)), ((), ())),
                    preferred_element_type=F32,
                )
                state = jnp.concatenate([both[:HDIM, :HDIM], both[HDIM:, HDIM:]], axis=0)
                idx = r * per_tile + c
                if idx == 0:
                    within[i, 0] = jnp.zeros_like(state)
                    run[...] = state
                else:
                    sofar = run[...]
                    within[i, idx] = sofar
                    run[...] = sofar + state

    causal = lax.broadcasted_iota(jnp.int32, (CHUNK, CHUNK), 0) >= lax.broadcasted_iota(
        jnp.int32, (CHUNK, CHUNK), 1
    )

    def qa_stage(i):
        cs = slice(i * PAIR, (i + 1) * PAIR)
        w_copy(2, i).wait()
        for r in range(tiles):
            rs = slice(r * TILE, (r + 1) * TILE)
            query = silu(dot(tok[rs, :], wq[:, cs])).astype(BF16)
            q_v[rs, cs] = query
            for c in range(per_tile):
                at = slice(r * TILE + c * CHUNK, r * TILE + (c + 1) * CHUNK)
                for h in range(2):
                    hs = slice(i * PAIR + h * HDIM, i * PAIR + (h + 1) * HDIM)
                    s = lax.dot_general(
                        query[c * CHUNK : (c + 1) * CHUNK, h * HDIM : (h + 1) * HDIM],
                        k_v[at, hs],
                        (((1,), (1,)), ((), ())),
                        preferred_element_type=F32,
                    )
                    s = jnp.where(causal, s, 0.0).astype(BF16)
                    att[at, hs] = dot(s, v_v[at, hs])

    def n_copy(i, c):
        part = (pl.ds(c * CHUNK, CHUNK), pl.ds(i * PAIR, PAIR))
        return pltpu.make_async_remote_copy(
            src_ref=normed.at[part],
            dst_ref=normed_peer.at[part],
            send_sem=sn.at[i, c],
            recv_sem=rn.at[i, c],
            device_id={"tp": peer},
            device_id_type=MESH,
        )

    def c_stage(i):
        p3_finish(i)
        prefix = p3_recv[i].reshape(PAIR, HDIM).astype(F32)
        cs = slice(i * PAIR, (i + 1) * PAIR)
        zero = jnp.zeros((HDIM, HDIM), BF16)
        for c in range(rows // CHUNK):
            at = slice(c * CHUNK, (c + 1) * CHUNK)
            carried = (prefix + within[i, c]).astype(BF16)
            diag = jnp.concatenate(
                [
                    jnp.concatenate([carried[:HDIM], zero], axis=1),
                    jnp.concatenate([zero, carried[HDIM:]], axis=1),
                ],
                axis=0,
            )
            full = att[at, cs] + dot(q_v[at, cs], diag)
            for h in range(2):
                x = full[:, h * HDIM : (h + 1) * HDIM]
                meansq = jnp.mean(x * x, axis=-1, keepdims=True)
                hs = slice(i * PAIR + h * HDIM, i * PAIR + (h + 1) * HDIM)
                normed[at, hs] = (x * lax.rsqrt(meansq + 1e-06)).astype(BF16)
            n_copy(i, c).start()

    kv_stage(0)
    pl.semaphore_wait(barrier, GROUP - 1 + groups - 1 + 1)
    p1_start(0)
    wo_remote.start()
    kv_stage(1)
    p1_start(1)
    p1_finish(0)
    kv_stage(2)
    p1_start(2)
    p2_finish(0)
    p1_finish(1)
    qa_stage(0)
    p2_finish(1)
    p1_finish(2)
    qa_stage(1)
    p2_finish(2)
    qa_stage(2)
    for i in range(pairs):
        c_stage(i)

    wo_copy.wait()
    for r in range(tiles):
        rs = slice(r * TILE, (r + 1) * TILE)
        acc[rs, :] = dot(normed[rs, :], wo_own[...])
    wo_remote.wait_recv()

    def out_copy(c):
        part = pl.ds(c * CHUNK, CHUNK)
        return pltpu.make_async_copy(out_v.at[part], out_hbm.at[part], out_sem.at[c])

    for c in range(rows // CHUNK):
        at = slice(c * CHUNK, (c + 1) * CHUNK)
        for i in range(pairs):
            n_copy(i, c).wait_recv()
        out_v[at, :] = (acc[at, :] + dot(normed_peer[at, :], wo_peer[...])).astype(BF16)
        out_copy(c).start()

    wo_remote.wait_send()
    for i in range(pairs):
        for k in range(1, GROUP):
            p1_copy(i, k, p, after(k)).wait_send()
            p3_copy(i, k, p, after(k)).wait_send()
        for to in range(1, groups):

            @pl.when(to > g)
            def _():
                p2_copy(i, g, to).wait_send()

        for c in range(rows // CHUNK):
            n_copy(i, c).wait_send()
    for c in range(rows // CHUNK):
        out_copy(c).wait()


def body(n_ctx, tokens, w_query, w_key, w_value, w_out):
    rows, width = tokens.shape
    cols = w_query.shape[1]
    out_cols = w_out.shape[1] // 2
    pairs = cols // PAIR
    chunks = rows // CHUNK
    groups = n_ctx // GROUP
    quarter = PAIR // GROUP
    dma = pltpu.SemaphoreType.DMA
    vmem = pltpu.VMEM
    return pl.pallas_call(
        functools.partial(kernel, n_ctx),
        out_shape=jax.ShapeDtypeStruct((rows, out_cols), BF16),
        in_specs=[pl.BlockSpec(memory_space=pl.ANY)] * 5,
        out_specs=pl.BlockSpec(memory_space=pl.ANY),
        scratch_shapes=[
            vmem((rows, width), BF16),
            vmem((width, cols), BF16),
            vmem((width, cols), BF16),
            vmem((width, cols), BF16),
            vmem((cols, out_cols), BF16),
            vmem((cols, out_cols), BF16),
            vmem((rows, cols), BF16),
            vmem((rows, cols), BF16),
            vmem((rows, cols), BF16),
            vmem((rows, cols), F32),
            vmem((pairs, chunks, PAIR, HDIM), F32),
            vmem((PAIR, HDIM), F32),
            vmem((rows, cols), BF16),
            vmem((rows, cols), BF16),
            vmem((rows, out_cols), F32),
            vmem((rows, out_cols), BF16),
            vmem((pairs, GROUP, quarter, HDIM), BF16),
            vmem((pairs, GROUP, quarter, HDIM), BF16),
            vmem((pairs, quarter, HDIM), BF16),
            vmem((pairs, groups, quarter, HDIM), BF16),
            vmem((pairs, GROUP, quarter, HDIM), BF16),
            vmem((pairs, GROUP, quarter, HDIM), BF16),
            dma((rows // TILE,)),
            dma((3, pairs)),
            dma,
            dma((chunks,)),
            dma,
            dma,
            dma((pairs, GROUP)),
            dma((pairs, GROUP)),
            dma((pairs, groups)),
            dma((pairs, groups)),
            dma((pairs, GROUP)),
            dma((pairs, GROUP)),
            dma((pairs, chunks)),
            dma((pairs, chunks)),
        ],
        compiler_params=pltpu.CompilerParams(
            collective_id=0, has_side_effects=True, vmem_limit_bytes=56 * 1024 * 1024
        ),
        cost_estimate=pl.CostEstimate(
            flops=2 * rows * (3 * width * cols + 2 * cols * out_cols + 4 * CHUNK * cols),
            bytes_accessed=2 * (rows * width + 5 * width * cols),
            transcendentals=2 * rows * cols,
        ),
    )(tokens, w_query, w_key, w_value, w_out)


def solution(mesh):
    return jax.shard_map(
        functools.partial(body, mesh.shape["ctx"]),
        mesh=mesh,
        in_specs=(P("ctx", None), P(None, "tp"), P(None, "tp"), P(None, "tp"), P("tp", None)),
        out_specs=P("ctx", "tp"),
        check_vma=False,
    )
```

time: 187 us -> 37.2 us (0.20)
  waiting for transfers between devices: 106 us -> 0 us
  matrix products: 37.3 us -> 0 us
  Pallas kernels: 0 us -> 34.4 us
  local copies, waits for them, and re-layouts: 23 us -> 2.65 us
  between operations: 13.5 us -> 0.01 us
  other arithmetic: 4.99 us -> 0 us
    all_gather x1 -> x0, waiting for transfers between devices: 76.7 us -> none  [carried_in(): gathered = lax.all_gather(part, axis)]
    dot_general x7 -> x0, matrix products: 37.3 us -> none  [the longest x1 8.26 us: body(): jnp.einsum('bhst,bthe->bshe', scores, values, preferred_element_type=jnp....]
    pallas_call x0 -> x1, Pallas kernels: none -> 34.4 us  [body(): pl.pallas_call(functools.partial(kernel, n_ctx), out_shape=jax.ShapeDtype...]
    reduce_scatter x1 -> x0, waiting for transfers between devices: 29.7 us -> none  [body(): lax.psum_scatter(partial_out, 'tp', scatter_dimension=1, tiled=True)]
    reshape x4 -> x0, local copies, waits for them, and re-layouts: 17.1 us -> none  [the longest x2 8.41 us: body(): keys = keys.reshape(count, BLK, heads_here, HDIM)]
    convert_element_type x2 -> x0, other arithmetic: 3.67 us -> none  [the longest x1 3.18 us: body(): lax.psum_scatter(partial_out, 'tp', scatter_dimension=1, tiled=True)]
  transfers between devices with their start and end apart: 2 -> 0, of which waited for: 2 -> 0; matrix products, arithmetic and copies ran while one was open for 11% -> 0% of each run, Pallas kernels for 0% -> 0%
where the time goes in v1:
time: 37.2 us; the launch traced here: 37.1 us
  Pallas kernels  34.4 us (92%)
  local copies, waits for them, and re-layouts  2.65 us (7%)
    pallas_call x1, Pallas kernels, body(): pl.pallas_call(functools.partial(kernel, n_ctx), out_shape=jax.ShapeDtype...  34.4 us
    unnamed x1, local copies, waits for them, and re-layouts  2.65 us

profile of v1, /device:TPU:0, one launch (start us, length us, event | category | flops | bytes accessed | tf_op | source)
XLA Modules:
  0.0 37.1 jit_solution(14966508404395308046)
XLA Ops:
  0.0 34.4 %shard_map.55 = bf16[1024,768]{1,0:T(8,128)(2,1)} custom-call(bf16[1024,1536]{1,0:T(8,128)(2,1)} %tok_hbm.1, bf16[1536,768]{1,0:T(8,128)(2,1)} %wq_hbm.1, bf16[1536,768]{1,0:T(8,128)(2,1)} %wk_hbm.1, bf16[1536,768]{1,0:T(8,128)(2,1)} %wv_hbm.1, bf16[768,1536]{1,0:T(8,128)(2,1)} %wo_hbm.1), custom_call_target="tpu_custom_call" | custom-call | flops 11274289152 | bytes 14942208 | tf_op jit(solution)/shard_map/pallas_call | solution.py:373
  34.4 2.7 %copy.7 = bf16[1024,768]{1,0:T(8,128)(2,1)} copy(bf16[1024,768]{1,0:T(8,128)(2,1)} %shard_map.55) | data formatting | bytes 3145728

commit v2 on v1

--- a/solution.py
+++ b/solution.py
@@ -127,14 +127,6 @@
     w_copy(0, 0).start()
     tok_copy(0).start()
     w_copy(1, 0).start()
-    for r in range(1, tiles):
-        tok_copy(r).start()
-    for i in range(1, pairs):
-        w_copy(0, i).start()
-        w_copy(1, i).start()
-    for i in range(pairs):
-        w_copy(2, i).start()
-    wo_copy.start()
 
     def p1_copy(i, k, slot, to):
         return pltpu.make_async_remote_copy(
@@ -223,6 +215,12 @@
         for r in range(tiles):
             if i == 0:
                 tok_copy(r).wait()
+                if r == 0:
+                    for later in range(1, tiles):
+                        tok_copy(later).start()
+                if r == tiles - 1:
+                    w_copy(0, 1).start()
+                    w_copy(1, 1).start()
             rs = slice(r * TILE, (r + 1) * TILE)
             keys = silu(dot(tok[rs, :], wk[:, cs])).astype(BF16)
             k_v[rs, cs] = keys
@@ -252,25 +250,27 @@
         jnp.int32, (CHUNK, CHUNK), 1
     )
 
-    def qa_stage(i):
+    def q_stage(i):
         cs = slice(i * PAIR, (i + 1) * PAIR)
         w_copy(2, i).wait()
         for r in range(tiles):
             rs = slice(r * TILE, (r + 1) * TILE)
-            query = silu(dot(tok[rs, :], wq[:, cs])).astype(BF16)
-            q_v[rs, cs] = query
-            for c in range(per_tile):
-                at = slice(r * TILE + c * CHUNK, r * TILE + (c + 1) * CHUNK)
-                for h in range(2):
-                    hs = slice(i * PAIR + h * HDIM, i * PAIR + (h + 1) * HDIM)
-                    s = lax.dot_general(
-                        query[c * CHUNK : (c + 1) * CHUNK, h * HDIM : (h + 1) * HDIM],
-                        k_v[at, hs],
-                        (((1,), (1,)), ((), ())),
-                        preferred_element_type=F32,
-                    )
-                    s = jnp.where(causal, s, 0.0).astype(BF16)
-                    att[at, hs] = dot(s, v_v[at, hs])
+            q_v[rs, cs] = silu(dot(tok[rs, :], wq[:, cs])).astype(BF16)
+
+    def attn_stage(c):
+        at = slice(c * CHUNK, (c + 1) * CHUNK)
+        heads = [slice(h * HDIM, (h + 1) * HDIM) for h in range(cols // HDIM)]
+        scores = []
+        for hs in heads:
+            s = lax.dot_general(
+                q_v[at, hs],
+                k_v[at, hs],
+                (((1,), (1,)), ((), ())),
+                preferred_element_type=F32,
+            )
+            scores.append(jnp.where(causal, s, 0.0).astype(BF16))
+        for hs, s in zip(heads, scores):
+            att[at, hs] = dot(s, v_v[at, hs])
 
     def n_copy(i, c):
         part = (pl.ds(c * CHUNK, CHUNK), pl.ds(i * PAIR, PAIR))
@@ -307,29 +307,43 @@
             n_copy(i, c).start()
 
     kv_stage(0)
+    for i in range(2, pairs):
+        w_copy(0, i).start()
+        w_copy(1, i).start()
     pl.semaphore_wait(barrier, GROUP - 1 + groups - 1 + 1)
     p1_start(0)
-    wo_remote.start()
     kv_stage(1)
+    for i in range(pairs):
+        w_copy(2, i).start()
     p1_start(1)
     p1_finish(0)
+    wo_remote.start()
+    wo_copy.start()
     kv_stage(2)
     p1_start(2)
     p2_finish(0)
     p1_finish(1)
-    qa_stage(0)
+    q_stage(0)
+    q_stage(1)
     p2_finish(1)
     p1_finish(2)
-    qa_stage(1)
+    q_stage(2)
+    attn_stage(0)
+    attn_stage(1)
     p2_finish(2)
-    qa_stage(2)
-    for i in range(pairs):
-        c_stage(i)
-
+    for c in range(2, rows // CHUNK):
+        attn_stage(c)
+    c_stage(0)
+    c_stage(1)
     wo_copy.wait()
+    early = (pairs - 1) * PAIR
     for r in range(tiles):
         rs = slice(r * TILE, (r + 1) * TILE)
-        acc[rs, :] = dot(normed[rs, :], wo_own[...])
+        acc[rs, :] = dot(normed[rs, :early], wo_own[:early, :])
+    c_stage(2)
+    for r in range(tiles):
+        rs = slice(r * TILE, (r + 1) * TILE)
+        acc[rs, :] += dot(normed[rs, early:], wo_own[early:, :])
     wo_remote.wait_recv()
 
     def out_copy(c):

time: 37.2 us -> 32 us (0.86)
  Pallas kernels: 34.4 us -> 29.2 us
    pallas_call x1, Pallas kernels: 34.4 us -> 29.2 us  [body(): pl.pallas_call(functools.partial(kernel, n_ctx), out_shape=jax.ShapeDtype...]
where the time goes in v2:
time: 32 us; the launch traced here: 31.9 us
  Pallas kernels  29.2 us (91%)
  local copies, waits for them, and re-layouts  2.65 us (8%)
    pallas_call x1, Pallas kernels, body(): pl.pallas_call(functools.partial(kernel, n_ctx), out_shape=jax.ShapeDtype...  29.2 us
    unnamed x1, local copies, waits for them, and re-layouts  2.65 us

profile of v2, /device:TPU:0, one launch (start us, length us, event | category | flops | bytes accessed | tf_op | source)
XLA Modules:
  0.0 31.9 jit_solution(8509481031878653802)
XLA Ops:
  0.0 29.2 %shard_map.55 = bf16[1024,768]{1,0:T(8,128)(2,1)} custom-call(bf16[1024,1536]{1,0:T(8,128)(2,1)} %tok_hbm.1, bf16[1536,768]{1,0:T(8,128)(2,1)} %wq_hbm.1, bf16[1536,768]{1,0:T(8,128)(2,1)} %wk_hbm.1, bf16[1536,768]{1,0:T(8,128)(2,1)} %wv_hbm.1, bf16[768,1536]{1,0:T(8,128)(2,1)} %wo_hbm.1), custom_call_target="tpu_custom_call" | custom-call | flops 11274289152 | bytes 14942208 | tf_op jit(solution)/shard_map/pallas_call | solution.py:387
  29.2 2.7 %copy.7 = bf16[1024,768]{1,0:T(8,128)(2,1)} copy(bf16[1024,768]{1,0:T(8,128)(2,1)} %shard_map.55) | data formatting | bytes 3145728

commit v3 on v2

--- a/solution.py
+++ b/solution.py
@@ -32,7 +32,7 @@
     wk_hbm,
     wv_hbm,
     wo_hbm,
-    out_hbm,
+    out,
     tok,
     wq,
     wk,
@@ -48,7 +48,6 @@
     normed,
     normed_peer,
     acc,
-    out_v,
     p1_send,
     p1_recv,
     p2_send,
@@ -58,7 +57,6 @@
     tok_sem,
     w_sem,
     wo_sem,
-    out_sem,
     wo_ssem,
     wo_rsem,
     s1,
@@ -325,37 +323,38 @@
     p1_finish(1)
     q_stage(0)
     q_stage(1)
+    q_stage(2)
     p2_finish(1)
     p1_finish(2)
-    q_stage(2)
     attn_stage(0)
     attn_stage(1)
+    attn_stage(2)
     p2_finish(2)
-    for c in range(2, rows // CHUNK):
+    for c in range(3, rows // CHUNK):
         attn_stage(c)
     c_stage(0)
     c_stage(1)
     wo_copy.wait()
+    wo_remote.wait_recv()
     early = (pairs - 1) * PAIR
     for r in range(tiles):
         rs = slice(r * TILE, (r + 1) * TILE)
         acc[rs, :] = dot(normed[rs, :early], wo_own[:early, :])
+    for r in range(tiles):
+        rs = slice(r * TILE, (r + 1) * TILE)
+        for c in range(r * per_tile, (r + 1) * per_tile):
+            for i in range(pairs - 1):
+                n_copy(i, c).wait_recv()
+        acc[rs, :] += dot(normed_peer[rs, :early], wo_peer[:early, :])
     c_stage(2)
     for r in range(tiles):
         rs = slice(r * TILE, (r + 1) * TILE)
         acc[rs, :] += dot(normed[rs, early:], wo_own[early:, :])
-    wo_remote.wait_recv()
-
-    def out_copy(c):
-        part = pl.ds(c * CHUNK, CHUNK)
-        return pltpu.make_async_copy(out_v.at[part], out_hbm.at[part], out_sem.at[c])
 
     for c in range(rows // CHUNK):
         at = slice(c * CHUNK, (c + 1) * CHUNK)
-        for i in range(pairs):
-            n_copy(i, c).wait_recv()
-        out_v[at, :] = (acc[at, :] + dot(normed_peer[at, :], wo_peer[...])).astype(BF16)
-        out_copy(c).start()
+        n_copy(pairs - 1, c).wait_recv()
+        out[at, :] = (acc[at, :] + dot(normed_peer[at, early:], wo_peer[early:, :])).astype(BF16)
 
     wo_remote.wait_send()
     for i in range(pairs):
@@ -370,8 +369,6 @@
 
         for c in range(rows // CHUNK):
             n_copy(i, c).wait_send()
-    for c in range(rows // CHUNK):
-        out_copy(c).wait()
 
 
 def body(n_ctx, tokens, w_query, w_key, w_value, w_out):
@@ -386,9 +383,9 @@
     vmem = pltpu.VMEM
     return pl.pallas_call(
         functools.partial(kernel, n_ctx),
-        out_shape=jax.ShapeDtypeStruct((rows, out_cols), BF16),
+        out_shape=pltpu.VMEM((rows, out_cols), BF16),
         in_specs=[pl.BlockSpec(memory_space=pl.ANY)] * 5,
-        out_specs=pl.BlockSpec(memory_space=pl.ANY),
+        out_specs=pl.BlockSpec(memory_space=pltpu.VMEM),
         scratch_shapes=[
             vmem((rows, width), BF16),
             vmem((width, cols), BF16),
@@ -405,7 +402,6 @@
             vmem((rows, cols), BF16),
             vmem((rows, cols), BF16),
             vmem((rows, out_cols), F32),
-            vmem((rows, out_cols), BF16),
             vmem((pairs, GROUP, quarter, HDIM), BF16),
             vmem((pairs, GROUP, quarter, HDIM), BF16),
             vmem((pairs, quarter, HDIM), BF16),
@@ -415,7 +411,6 @@
             dma((rows // TILE,)),
             dma((3, pairs)),
             dma,
-            dma((chunks,)),
             dma,
             dma,
             dma((pairs, GROUP)),

time: 32 us -> 29.1 us (0.909)
  local copies, waits for them, and re-layouts: 2.65 us -> 1.15 us
  Pallas kernels: 29.2 us -> 27.8 us
    unnamed x1, local copies, waits for them, and re-layouts: 2.65 us -> 1.15 us
    pallas_call x1, Pallas kernels: 29.2 us -> 27.8 us  [body(): pl.pallas_call(functools.partial(kernel, n_ctx), out_shape=pltpu.VMEM((ro...]
where the time goes in v3:
time: 29.1 us; the launch traced here: 28.9 us
  Pallas kernels  27.8 us (96%)
  local copies, waits for them, and re-layouts  1.15 us (4%)
    pallas_call x1, Pallas kernels, body(): pl.pallas_call(functools.partial(kernel, n_ctx), out_shape=pltpu.VMEM((ro...  27.8 us
    unnamed x1, local copies, waits for them, and re-layouts  1.15 us

profile of v3, /device:TPU:0, one launch (start us, length us, event | category | flops | bytes accessed | tf_op | source)
XLA Modules:
  0.0 28.9 jit_solution(17314395231733330681)
XLA Ops:
  0.0 27.8 %shard_map.55 = bf16[1024,768]{1,0:T(8,128)(2,1)S(1)} custom-call(bf16[1024,1536]{1,0:T(8,128)(2,1)} %tok_hbm.1, bf16[1536,768]{1,0:T(8,128)(2,1)} %wq_hbm.1, bf16[1536,768]{1,0:T(8,128)(2,1)} %wk_hbm.1, bf16[1536,768]{1,0:T(8,128)(2,1)} %wv_hbm.1, bf16[768,1536]{1,0:T(8,128)(2,1)} %wo_hbm.1), custom_call_target="tpu_custom_call" | custom-call | flops 11274289152 | bytes 14942208 | tf_op jit(solution)/shard_map/pallas_call | solution.py:384
  27.8 1.1 %copy.7 = bf16[1024,768]{1,0:T(8,128)(2,1)} copy(bf16[1024,768]{1,0:T(8,128)(2,1)S(1)} %shard_map.55) | data formatting | bytes 3145728
